TPU v7x, 32 devices: a whole 2x2x4 slice. The times are simulated.
32 devices in a mesh: tilt: 4 (over z), pos: 8 (over y, x, core).
Axes of the slice: x: 2, y: 2, z: 4, core: 2. Of those that a mesh axis runs over, the one named last changes fastest.
Arguments:
- intensity: bfloat16 [4, 128, 256, 256], P('tilt', 'pos'), may hold values from 0 to 1
- positions: int32 [4, 128, 2], P('tilt', 'pos'), may hold values from 0 to 512, as said below
- counts: int32 [4, 8], P('tilt', 'pos'), may hold values from 8 to 16, as said below
- object_field: bfloat16 [4, 2, 768, 768], P('tilt', None, 'pos'), may hold values from 0.5 to 1.5
- probe: float32 [2, 256, 256], replicated, may hold values from -3 to 3
Outputs:
- object_grad: float32 [4, 2, 768, 768], P('tilt', None, 'pos')
- probe_grad: float32 [2, 256, 256], replicated
Inputs may be any that keep to these rules, and one draw needn't show every extreme that they name: The batch pairs each flat tilt t < 2 with the steep tilt t + 2: for every position index p, counts[t, p] + counts[t + 2, p] = 24 and counts[t, p] <= 12. `positions`: the row offset of a slot of position index p lies between max(0, (p - 2) * 96) and min(512, (p + 256 // 96 + 1) * 96 - 256); column offsets lie between 0 and 512.
All inputs are finite; a program needn't handle non-finite values.
Results may differ from a plain program's by a relative error of at most 0.0017.
The roundings to bfloat16 on the way count: a program that leaves them out, or rounds other values in their place, can miss the bound.
Values may be sent and summed in bfloat16 or wider, within the bound.
A program may use at most 128 MiB of HBM per device.

v0:
```python
import math

import jax
import jax.numpy as jnp
from jax import lax
from jax.sharding import PartitionSpec as P


def dft_tables(length):
    index = jnp.arange(length, dtype=jnp.int32)
    phase = (index[:, None] * index[None, :] % length).astype(jnp.float32) * (
        2.0 * math.pi / length
    )
    cosine = jnp.cos(phase) / math.sqrt(length)
    sine = jnp.sin(phase) / math.sqrt(length)
    forward_table = jnp.stack([jnp.stack([cosine, -sine]), jnp.stack([sine, cosine])]).astype(
        jnp.bfloat16
    )
    inverse_table = jnp.stack([jnp.stack([cosine, sine]), jnp.stack([-sine, cosine])]).astype(
        jnp.bfloat16
    )
    return (forward_table, inverse_table)


def along_columns(field, table):
    return jnp.einsum("fcry,cdyk->fdrk", field, table, preferred_element_type=jnp.float32)


def along_rows(field, table):
    return jnp.einsum("fcyk,cdyr->fdrk", field, table, preferred_element_type=jnp.float32)


def frame_grads(frames, patches, probe, forward_table, inverse_table, live):
    probe_re, probe_im = (probe[0], probe[1])
    patch_re = patches[:, 0].astype(jnp.float32)
    patch_im = patches[:, 1].astype(jnp.float32)
    exit_wave = jnp.stack(
        [probe_re * patch_re - probe_im * patch_im, probe_re * patch_im + probe_im * patch_re], 1
    ).astype(jnp.bfloat16)
    half = along_columns(exit_wave, forward_table).astype(jnp.bfloat16)
    far = along_rows(half, forward_table)
    misfit = far[:, 0] * far[:, 0] + far[:, 1] * far[:, 1] - frames.astype(jnp.float32)
    back = (far * misfit[:, None]).astype(jnp.bfloat16)
    middle = along_rows(back, inverse_table).astype(jnp.bfloat16)
    wave = along_columns(middle, inverse_table)
    wave_re, wave_im = (wave[:, 0], wave[:, 1])
    grads = jnp.stack(
        [probe_re * wave_re + probe_im * wave_im, probe_re * wave_im - probe_im * wave_re], 1
    ).astype(jnp.bfloat16)
    grads = jnp.where(live[:, None, None, None], grads, jnp.zeros_like(grads))
    weight = live.astype(jnp.float32)[:, None, None]
    numer_re = jnp.sum((patch_re * wave_re + patch_im * wave_im) * weight, axis=0)
    numer_im = jnp.sum((patch_re * wave_im - patch_im * wave_re) * weight, axis=0)
    denom = jnp.sum((patch_re * patch_re + patch_im * patch_im) * weight, axis=0)
    return (grads, jnp.stack([numer_re, numer_im]), denom)


def column_picker(column, width, columns):
    full = jnp.arange(columns, dtype=jnp.int32)
    inner = jnp.arange(width, dtype=jnp.int32)
    return (full[:, None] == inner[None, :] + column).astype(jnp.bfloat16)


def cut_patches(image, places, width):
    columns = image.shape[2]
    zero = jnp.zeros((), jnp.int32)

    def cut_one(place):
        band = lax.dynamic_slice(image, (zero, place[0], zero), (2, width, columns))
        picker = column_picker(place[1], width, columns)
        return jnp.einsum("crx,xk->crk", band, picker, preferred_element_type=jnp.float32).astype(
            jnp.bfloat16
        )

    return lax.map(cut_one, places)


def place_patches(total, pieces, places, keep):
    width = pieces.shape[-1]
    columns = total.shape[2]
    zero = jnp.zeros((), jnp.int32)

    def add_one(index, total):
        piece = jnp.where(keep[index], pieces[index], jnp.zeros((), jnp.bfloat16))
        picker = column_picker(places[index, 1], width, columns)
        spread = jnp.einsum("crk,xk->crx", piece, picker, preferred_element_type=jnp.float32)
        start = (zero, places[index, 0], zero)
        current = lax.dynamic_slice(total, start, (2, width, columns))
        return lax.dynamic_update_slice(total, current + spread, start)

    return lax.fori_loop(0, pieces.shape[0], add_one, total)


def local(intensity, positions, counts, object_field, probe):
    width = probe.shape[-1]
    slots = intensity.shape[1]
    image = lax.all_gather(object_field, "pos", axis=2, tiled=True)[0]
    forward_table, inverse_table = dft_tables(width)
    own_places = positions[0]
    own_frames = intensity[0]
    own_patches = cut_patches(image, own_places, width)
    slot_index = jnp.arange(slots, dtype=jnp.int32)
    live = slot_index < counts[0, 0]
    grads, numer, denom = frame_grads(
        own_frames, own_patches, probe, forward_table, inverse_table, live
    )
    pieces, places, keep = (grads, own_places, live)
    numer_all, denom_all = lax.psum((numer, denom), ("tilt", "pos"))
    probe_grad = numer_all / denom_all[None]
    total = place_patches(jnp.zeros(image.shape, jnp.float32), pieces, places, keep)
    object_grad = lax.psum_scatter(total[None], "pos", scatter_dimension=2, tiled=True)
    return (object_grad, probe_grad)


def solution(mesh):
    placed = (
        P("tilt", "pos", None, None),
        P("tilt", "pos", None),
        P("tilt", "pos"),
        P("tilt", None, "pos", None),
        P(),
    )
    return jax.shard_map(
        local,
        mesh=mesh,
        in_specs=placed,
        out_specs=(P("tilt", None, "pos", None), P()),
        check_vma=False,
    )
```

profile of v0, /device:TPU:0, one launch (start us, length us, event | category | flops | bytes accessed | tf_op | source)
XLA Modules:
  0.0 434.5 jit_solution(15960235231001083799)
XLA Ops:
  8.0 1.1 slice_bitcast_fusion.1
  11.0 1.1 negate_convert_fusion
  12.9 28.7 %all-gather.2.cloned.1.call-done = bf16[1,2,768,768]{3,2,1,0:T(8,128)(2,1)} async-done(((bf16[1,2,96,768]{3,2,1,0:T(8,128)(2,1)}), bf16[1,2,768,768]{3,2,1,0:T(8,128)(2,1)}) %all-gather.2.cloned.1.call-update) | async-done | bytes 2359312 | tf_op jit(solution)/shard_map/all_gather | solution.py:97
  41.7 87.0 %while.25 = (s32[]{:T(128)}, bf16[16,2,256,256]{2,3,0,1:T(8,128)(2,1)}, s32[16,2]{0,1:T(2,128)S(1)}, bf16[2,768,768]{2,1,0:T(8,128)(2,1)}) while((s32[]{:T(128)}, bf16[16,2,256,256]{2,3,0,1:T(8,128)(2,1)}, s32[16,2]{0,1:T(2,128)S(1)}, bf16[2,768,768]{2,1,0:T(8,128)(2,1)}) %tuple.90), condition=%wide.region_1.2_spmd.clone, body=%wide.region_0.1_spmd.sunk.clone | while | flops 201654528 | bytes 2099843 | solution.py:75
  44.6 1.6 fusion.97
  50.0 1.6 fusion.97
  55.5 1.6 fusion.97
  60.9 1.6 fusion.97
  66.3 1.6 fusion.97
  71.8 1.6 fusion.97
  77.2 1.6 fusion.97
  82.6 1.6 fusion.97
  88.1 1.6 fusion.97
  93.5 1.6 fusion.97
  98.9 1.6 fusion.97
  104.4 1.6 fusion.97
  109.8 1.6 fusion.97
  115.3 1.6 fusion.97
  120.7 1.6 fusion.97
  126.2 1.6 fusion.97
  128.7 5.5 %fusion.15 = (bf16[16,1,256,256]{2,3,0,1:T(8,128)(2,1)}, bf16[16,1,256,256]{2,3,0,1:T(8,128)(2,1)}) fusion(f32[256,256]{0,1:T(8,128)S(1)} %copy.19, f32[256,256]{0,1:T(8,128)S(1)} %copy.15, bf16[16,2,256,256]{2,3,0,1:T(8,128)(2,1)} %get-tuple-element.118), kind=kLoop, calls=%fused_computation.37 | loop fusion | flops 10485760 | bytes 8912896 | tf_op jit(solution)/shard_map/convert.3
  134.2 10.3 %fusion.48 = f32[16,2,256,256]{3,2,0,1:T(8,128)} fusion(bf16[1,2,256,256]{2,3,0,1:T(8,128)(2,1)} %get-tuple-element.178, bf16[1,2,256,256]{2,3,0,1:T(8,128)(2,1)S(1)} %get-tuple-element.173, bf16[16,1,256,256]{2,3,0,1:T(8,128)(2,1)} %get-tuple-element.170, bf16[16,1,256,256]{2,3,0,1:T(8,128)(2,1)} %get-tuple-element.169), kind=kOutput, calls=%fused_computation.72 | convolution fusion | flops 4301258752 | bytes 13107200 | tf_op jit(solution)/shard_map/fcyk,cdyr->fdrk/dot_general | solution.py:30
  144.5 6.3 %fusion.39 = f32[16,256,256]{2,1,0:T(8,128)} fusion(f32[16,2,256,256]{3,2,0,1:T(8,128)} %fusion.48, bf16[1,16,256,256]{3,2,1,0:T(8,128)(2,1)S(1)} %copy-done.2), kind=kLoop, calls=%fused_computation.60 | loop fusion | flops 5242880 | bytes 14680064 | tf_op jit(solution)/shard_map/mul | solution.py:43
  150.8 9.6 %fusion.45 = f32[16,2,256,256]{2,3,0,1:T(8,128)} fusion(bf16[2,2,256,256,1]{2,3,1,0,4:T(8,128)(2,1)S(1)} %maximum_bitcast_fusion.1, f32[16,2,256,256]{3,2,0,1:T(8,128)} %fusion.48, f32[16,256,256]{2,1,0:T(8,128)} %fusion.39), kind=kOutput, calls=%fused_computation.71 | convolution fusion | flops 4301258752 | bytes 21495808 | tf_op jit(solution)/shard_map/fcry,cdyk->fdrk/dot_general | solution.py:26
  160.4 6.2 %add_convert_fusion = (bf16[16,1,256,256]{2,3,0,1:T(8,128)(2,1)S(1)}, bf16[16,1,256,256]{2,3,0,1:T(8,128)(2,1)}) fusion(f32[16,2,256,256]{2,3,0,1:T(8,128)} %fusion.45, f32[256,256]{0,1:T(8,128)S(1)} %copy.19, f32[256,256]{0,1:T(8,128)S(1)} %copy.15), kind=kLoop, calls=%fused_computation.70 | loop fusion | flops 8388608 | bytes 13107200 | tf_op jit(solution)/shard_map/convert.1
  166.6 1.6 copy-done.1
  168.2 3.2 fusion.21
  172.3 3.5 maximum_select_fusion
  175.8 2.4 broadcast_in_dim.40
  178.3 195.5 %while.26 = (s32[]{:T(128)}, f32[2,768,768]{2,1,0:T(8,128)}, s32[16,2]{0,1:T(2,128)S(1)}, pred[16]{0:T(512)(128)(4,1)S(1)}, bf16[16,2,256,256]{2,3,0,1:T(8,128)(2,1)}) while((s32[]{:T(128)}, f32[2,768,768]{2,1,0:T(8,128)}, s32[16,2]{0,1:T(2,128)S(1)}, pred[16]{0:T(512)(128)(4,1)S(1)}, bf16[16,2,256,256]{2,3,0,1:T(8,128)(2,1)}) %tuple.89), condition=%wide.region_3.4_spmd.clone, body=%wide.region_2.3_spmd.sunk.clone | while | flops 202047744 | bytes 7604362 | solution.py:91
  183.3 2.5 dynamic-slice_add_fusion.3
  185.8 4.7 %dynamic_update_slice.17 = f32[2,768,768]{2,1,0:T(8,128)} dynamic-update-slice(f32[2,768,768]{2,1,0:T(8,128)} %get-tuple-element.295, f32[2,256,768]{2,1,0:T(8,128)S(1)} %dynamic-slice_add_fusion.3, s32[]{:T(128)} %constant.66.clone.1..sunk.3, s32[]{:T(128)S(6)} %select_n.111, s32[]{:T(128)} %constant.66.clone.1..sunk.3) | dynamic-update-slice | bytes 3145732 | tf_op jit(solution)/shard_map/while/body/eval_jaxpr/dynamic_update_slice | solution.py:89
  195.5 2.5 dynamic-slice_add_fusion.3
  198.0 4.7 %dynamic_update_slice.17 = f32[2,768,768]{2,1,0:T(8,128)} dynamic-update-slice(f32[2,768,768]{2,1,0:T(8,128)} %get-tuple-element.295, f32[2,256,768]{2,1,0:T(8,128)S(1)} %dynamic-slice_add_fusion.3, s32[]{:T(128)} %constant.66.clone.1..sunk.3, s32[]{:T(128)S(6)} %select_n.111, s32[]{:T(128)} %constant.66.clone.1..sunk.3) | dynamic-update-slice | bytes 3145732 | tf_op jit(solution)/shard_map/while/body/eval_jaxpr/dynamic_update_slice | solution.py:89
  207.8 2.5 dynamic-slice_add_fusion.3
  210.2 4.7 %dynamic_update_slice.17 = f32[2,768,768]{2,1,0:T(8,128)} dynamic-update-slice(f32[2,768,768]{2,1,0:T(8,128)} %get-tuple-element.295, f32[2,256,768]{2,1,0:T(8,128)S(1)} %dynamic-slice_add_fusion.3, s32[]{:T(128)} %constant.66.clone.1..sunk.3, s32[]{:T(128)S(6)} %select_n.111, s32[]{:T(128)} %constant.66.clone.1..sunk.3) | dynamic-update-slice | bytes 3145732 | tf_op jit(solution)/shard_map/while/body/eval_jaxpr/dynamic_update_slice | solution.py:89
  220.0 2.5 dynamic-slice_add_fusion.3
  222.4 4.7 %dynamic_update_slice.17 = f32[2,768,768]{2,1,0:T(8,128)} dynamic-update-slice(f32[2,768,768]{2,1,0:T(8,128)} %get-tuple-element.295, f32[2,256,768]{2,1,0:T(8,128)S(1)} %dynamic-slice_add_fusion.3, s32[]{:T(128)} %constant.66.clone.1..sunk.3, s32[]{:T(128)S(6)} %select_n.111, s32[]{:T(128)} %constant.66.clone.1..sunk.3) | dynamic-update-slice | bytes 3145732 | tf_op jit(solution)/shard_map/while/body/eval_jaxpr/dynamic_update_slice | solution.py:89
  232.2 2.5 dynamic-slice_add_fusion.3
  234.7 4.7 %dynamic_update_slice.17 = f32[2,768,768]{2,1,0:T(8,128)} dynamic-update-slice(f32[2,768,768]{2,1,0:T(8,128)} %get-tuple-element.295, f32[2,256,768]{2,1,0:T(8,128)S(1)} %dynamic-slice_add_fusion.3, s32[]{:T(128)} %constant.66.clone.1..sunk.3, s32[]{:T(128)S(6)} %select_n.111, s32[]{:T(128)} %constant.66.clone.1..sunk.3) | dynamic-update-slice | bytes 3145732 | tf_op jit(solution)/shard_map/while/body/eval_jaxpr/dynamic_update_slice | solution.py:89
  244.4 2.5 dynamic-slice_add_fusion.3
  246.9 4.7 %dynamic_update_slice.17 = f32[2,768,768]{2,1,0:T(8,128)} dynamic-update-slice(f32[2,768,768]{2,1,0:T(8,128)} %get-tuple-element.295, f32[2,256,768]{2,1,0:T(8,128)S(1)} %dynamic-slice_add_fusion.3, s32[]{:T(128)} %constant.66.clone.1..sunk.3, s32[]{:T(128)S(6)} %select_n.111, s32[]{:T(128)} %constant.66.clone.1..sunk.3) | dynamic-update-slice | bytes 3145732 | tf_op jit(solution)/shard_map/while/body/eval_jaxpr/dynamic_update_slice | solution.py:89
  256.6 2.5 dynamic-slice_add_fusion.3
  259.1 4.7 %dynamic_update_slice.17 = f32[2,768,768]{2,1,0:T(8,128)} dynamic-update-slice(f32[2,768,768]{2,1,0:T(8,128)} %get-tuple-element.295, f32[2,256,768]{2,1,0:T(8,128)S(1)} %dynamic-slice_add_fusion.3, s32[]{:T(128)} %constant.66.clone.1..sunk.3, s32[]{:T(128)S(6)} %select_n.111, s32[]{:T(128)} %constant.66.clone.1..sunk.3) | dynamic-update-slice | bytes 3145732 | tf_op jit(solution)/shard_map/while/body/eval_jaxpr/dynamic_update_slice | solution.py:89
  268.9 2.5 dynamic-slice_add_fusion.3
  271.3 4.7 %dynamic_update_slice.17 = f32[2,768,768]{2,1,0:T(8,128)} dynamic-update-slice(f32[2,768,768]{2,1,0:T(8,128)} %get-tuple-element.295, f32[2,256,768]{2,1,0:T(8,128)S(1)} %dynamic-slice_add_fusion.3, s32[]{:T(128)} %constant.66.clone.1..sunk.3, s32[]{:T(128)S(6)} %select_n.111, s32[]{:T(128)} %constant.66.clone.1..sunk.3) | dynamic-update-slice | bytes 3145732 | tf_op jit(solution)/shard_map/while/body/eval_jaxpr/dynamic_update_slice | solution.py:89
  281.1 2.5 dynamic-slice_add_fusion.3
  283.6 4.7 %dynamic_update_slice.17 = f32[2,768,768]{2,1,0:T(8,128)} dynamic-update-slice(f32[2,768,768]{2,1,0:T(8,128)} %get-tuple-element.295, f32[2,256,768]{2,1,0:T(8,128)S(1)} %dynamic-slice_add_fusion.3, s32[]{:T(128)} %constant.66.clone.1..sunk.3, s32[]{:T(128)S(6)} %select_n.111, s32[]{:T(128)} %constant.66.clone.1..sunk.3) | dynamic-update-slice | bytes 3145732 | tf_op jit(solution)/shard_map/while/body/eval_jaxpr/dynamic_update_slice | solution.py:89
  293.3 2.5 dynamic-slice_add_fusion.3
  295.8 4.7 %dynamic_update_slice.17 = f32[2,768,768]{2,1,0:T(8,128)} dynamic-update-slice(f32[2,768,768]{2,1,0:T(8,128)} %get-tuple-element.295, f32[2,256,768]{2,1,0:T(8,128)S(1)} %dynamic-slice_add_fusion.3, s32[]{:T(128)} %constant.66.clone.1..sunk.3, s32[]{:T(128)S(6)} %select_n.111, s32[]{:T(128)} %constant.66.clone.1..sunk.3) | dynamic-update-slice | bytes 3145732 | tf_op jit(solution)/shard_map/while/body/eval_jaxpr/dynamic_update_slice | solution.py:89
  305.5 2.5 dynamic-slice_add_fusion.3
  308.0 4.7 %dynamic_update_slice.17 = f32[2,768,768]{2,1,0:T(8,128)} dynamic-update-slice(f32[2,768,768]{2,1,0:T(8,128)} %get-tuple-element.295, f32[2,256,768]{2,1,0:T(8,128)S(1)} %dynamic-slice_add_fusion.3, s32[]{:T(128)} %constant.66.clone.1..sunk.3, s32[]{:T(128)S(6)} %select_n.111, s32[]{:T(128)} %constant.66.clone.1..sunk.3) | dynamic-update-slice | bytes 3145732 | tf_op jit(solution)/shard_map/while/body/eval_jaxpr/dynamic_update_slice | solution.py:89
  317.8 2.5 dynamic-slice_add_fusion.3
  320.2 4.7 %dynamic_update_slice.17 = f32[2,768,768]{2,1,0:T(8,128)} dynamic-update-slice(f32[2,768,768]{2,1,0:T(8,128)} %get-tuple-element.295, f32[2,256,768]{2,1,0:T(8,128)S(1)} %dynamic-slice_add_fusion.3, s32[]{:T(128)} %constant.66.clone.1..sunk.3, s32[]{:T(128)S(6)} %select_n.111, s32[]{:T(128)} %constant.66.clone.1..sunk.3) | dynamic-update-slice | bytes 3145732 | tf_op jit(solution)/shard_map/while/body/eval_jaxpr/dynamic_update_slice | solution.py:89
  330.0 2.5 dynamic-slice_add_fusion.3
  332.5 4.7 %dynamic_update_slice.17 = f32[2,768,768]{2,1,0:T(8,128)} dynamic-update-slice(f32[2,768,768]{2,1,0:T(8,128)} %get-tuple-element.295, f32[2,256,768]{2,1,0:T(8,128)S(1)} %dynamic-slice_add_fusion.3, s32[]{:T(128)} %constant.66.clone.1..sunk.3, s32[]{:T(128)S(6)} %select_n.111, s32[]{:T(128)} %constant.66.clone.1..sunk.3) | dynamic-update-slice | bytes 3145732 | tf_op jit(solution)/shard_map/while/body/eval_jaxpr/dynamic_update_slice | solution.py:89
  342.2 2.5 dynamic-slice_add_fusion.3
  344.7 4.7 %dynamic_update_slice.17 = f32[2,768,768]{2,1,0:T(8,128)} dynamic-update-slice(f32[2,768,768]{2,1,0:T(8,128)} %get-tuple-element.295, f32[2,256,768]{2,1,0:T(8,128)S(1)} %dynamic-slice_add_fusion.3, s32[]{:T(128)} %constant.66.clone.1..sunk.3, s32[]{:T(128)S(6)} %select_n.111, s32[]{:T(128)} %constant.66.clone.1..sunk.3) | dynamic-update-slice | bytes 3145732 | tf_op jit(solution)/shard_map/while/body/eval_jaxpr/dynamic_update_slice | solution.py:89
  354.4 2.5 dynamic-slice_add_fusion.3
  356.9 4.7 %dynamic_update_slice.17 = f32[2,768,768]{2,1,0:T(8,128)} dynamic-update-slice(f32[2,768,768]{2,1,0:T(8,128)} %get-tuple-element.295, f32[2,256,768]{2,1,0:T(8,128)S(1)} %dynamic-slice_add_fusion.3, s32[]{:T(128)} %constant.66.clone.1..sunk.3, s32[]{:T(128)S(6)} %select_n.111, s32[]{:T(128)} %constant.66.clone.1..sunk.3) | dynamic-update-slice | bytes 3145732 | tf_op jit(solution)/shard_map/while/body/eval_jaxpr/dynamic_update_slice | solution.py:89
  366.6 2.5 dynamic-slice_add_fusion.3
  369.1 4.7 %dynamic_update_slice.17 = f32[2,768,768]{2,1,0:T(8,128)} dynamic-update-slice(f32[2,768,768]{2,1,0:T(8,128)} %get-tuple-element.295, f32[2,256,768]{2,1,0:T(8,128)S(1)} %dynamic-slice_add_fusion.3, s32[]{:T(128)} %constant.66.clone.1..sunk.3, s32[]{:T(128)S(6)} %select_n.111, s32[]{:T(128)} %constant.66.clone.1..sunk.3) | dynamic-update-slice | bytes 3145732 | tf_op jit(solution)/shard_map/while/body/eval_jaxpr/dynamic_update_slice | solution.py:89
  373.9 1.2 broadcast_divide_fusion
  376.0 51.9 %reduce-scatter.2.cloned.1.call-done = f32[1,2,96,768]{3,2,1,0:T(8,128)} async-done(((f32[1,2,768,768]{3,2,1,0:T(8,128)}), f32[1,2,96,768]{3,2,1,0:T(8,128)}) %reduce-scatter.2.cloned.1.call-update) | async-done | bytes 589840 | tf_op jit(solution)/shard_map/reduce_scatter | solution.py:111
  (183 shorter events, 86.1 us)
Async XLA Ops:
  7.2 34.5 %copy-start.3 = (s32[1,16,2]{1,2,0:T(2,128)S(1)}, s32[1,16,2]{1,2,0:T(2,128)}, u32[]{:S(2)}) copy-start(s32[1,16,2]{1,2,0:T(2,128)} %param.10) | copy-start | bytes 388
  7.2 34.5 %all-gather.2.cloned.1.call-start = ((), (), s32[]{:S(2)}) async-start(), calls=%async_computation.1 | async-start | bytes 2654208 | tf_op jit(solution)/shard_map/all_gather | solution.py:97
  7.9 365.9 %all-reduce.3.cloned.1.call-start = ((), (), s32[]{:S(2)}) async-start(), calls=%async_computation.3 | async-start | bytes 1572864 | tf_op jit(solution)/shard_map/psum | solution.py:108
  134.2 10.3 %copy-start.2 = (bf16[1,16,256,256]{3,2,1,0:T(8,128)(2,1)S(1)}, bf16[1,16,256,256]{3,2,1,0:T(8,128)(2,1)}, u32[]{:S(2)}) copy-start(bf16[1,16,256,256]{3,2,1,0:T(8,128)(2,1)} %param.9) | copy-start | bytes 6291460
  160.4 6.2 %copy-start = (f32[16,2,256,256]{2,3,0,1:T(8,128)S(1)}, f32[16,2,256,256]{2,3,0,1:T(8,128)}, u32[]{:S(2)}) copy-start(f32[16,2,256,256]{2,3,0,1:T(8,128)} %fusion.45) | copy-start | bytes 25165828
  160.4 7.8 %copy-start.1 = (bf16[16,2,256,256]{2,3,0,1:T(8,128)(2,1)S(1)}, bf16[16,2,256,256]{2,3,0,1:T(8,128)(2,1)}, u32[]{:S(2)}) copy-start(bf16[16,2,256,256]{2,3,0,1:T(8,128)(2,1)} %get-tuple-element.118) | copy-start | bytes 12582916
  172.2 255.7 %reduce-scatter.2.cloned.1.call-start = ((), (), s32[]{:S(2)}) async-start(), calls=%async_computation.2 | async-start | bytes 5308416 | tf_op jit(solution)/shard_map/reduce_scatter | solution.py:111
Sparse Core Ops, SparseCore 0:
  9.9 31.7 all-gather.1
  172.3 129.3 all-reduce.2
  373.9 53.9 reduce-scatter.1
where the time goes:
time: 439 us; the launch traced here: 434 us
  local copies, waits for them, and re-layouts  144 us (33%)
  matrix products  85.2 us (19%)
  waiting for transfers between devices  81.4 us (19%)
  loops' own time  60.4 us (14%)
  other arithmetic  49.2 us (11%)
  between operations  14.5 us (3%)
    dynamic_update_slice x16, local copies, waits for them, and re-layouts, add_one(): return lax.dynamic_update_slice(total, current + spread, start)  75.5 us
    reduce_scatter x1, waiting for transfers between devices, local(): lax.psum_scatter(total[None], 'pos', scatter_dimension=2, tiled=True)  51.9 us
    dot_general x16, matrix products, add_one(): jnp.einsum('crk,xk->crx', piece, picker, preferred_element_type=jnp.float32)  39.5 us
    another operation x1, loops' own time, place_patches(): return lax.fori_loop(0, pieces.shape[0], add_one, total)  32.7 us
    all_gather x1, waiting for transfers between devices, local(): image = lax.all_gather(object_field, 'pos', axis=2, tiled=True)[0]  28.7 us
    dynamic_slice x48, local copies, waits for them, and re-layouts, add_one(): piece = jnp.where(keep[index], pieces[index], jnp.zeros((), jnp.bfloat16))  27.7 us
    another operation x1, loops' own time, cut_patches(): return lax.map(cut_one, places)  27.7 us
    dot_general x16, matrix products, cut_one(): jnp.einsum('crx,xk->crk', band, picker, preferred_element_type=jnp.float32)  25.8 us
  transfers between devices with their start and end apart: 3, of which 2 were waited for; matrix products, arithmetic and copies ran while one was open for 40% of the time, Pallas kernels for 0%

commit v1 on v0

v1 whole, which is shorter than its diff:
```python
import functools

import jax
import jax.numpy as jnp
import numpy as np
from jax import lax
from jax.experimental import pallas as pl
from jax.experimental.pallas import tpu as pltpu
from jax.sharding import PartitionSpec as P

LANES = 128


def dft_tables(length):
    index = np.arange(length, dtype=np.int64)
    phase = (index[:, None] * index[None, :] % length).astype(np.float64) * (
        2.0 * np.pi / length
    )
    cosine = np.cos(phase) / np.sqrt(length)
    sine = np.sin(phase) / np.sqrt(length)
    forward = np.block([[cosine, -sine], [sine, cosine]])
    inverse = np.block([[cosine, sine], [-sine, cosine]])
    return (
        jnp.asarray(forward.astype(np.float32)).astype(jnp.bfloat16),
        jnp.asarray(inverse.astype(np.float32)).astype(jnp.bfloat16),
    )


def frames_kernel(
    reach,
    pos_ref,
    count_ref,
    frames_ref,
    *refs,
):
    blocks = 2 * reach + 1
    block_refs = refs[:blocks]
    probe_ref, fwd_ref, inv_ref = refs[blocks : blocks + 3]
    out_refs = refs[blocks + 3 : 2 * blocks + 3]
    sums_ref = refs[2 * blocks + 3]
    band, total = refs[2 * blocks + 4 :]
    rows = block_refs[0].shape[1]
    groups = block_refs[0].shape[2] // LANES
    width = probe_ref.shape[-1]
    wide = width // LANES

    for b in range(blocks):
        for c in range(2):
            for g in range(groups):
                band[c, g, pl.ds(b * rows, rows), :] = block_refs[b][
                    c, :, g * LANES : (g + 1) * LANES
                ].astype(jnp.float32)
    for c in range(2):
        band[c, groups] = jnp.zeros(band.shape[2:], jnp.float32)
    total[...] = jnp.zeros_like(total)
    sums_ref[...] = jnp.zeros_like(sums_ref)
    first = (lax.axis_index("pos") - reach) * rows

    def one_frame(i, carry):
        r = pos_ref[i, 0] - first
        q = pos_ref[i, 1]
        qb = q // LANES
        qs = q % LANES
        lane = lax.broadcasted_iota(jnp.int32, (width, LANES), 1)
        near = lane < LANES - qs
        back_shift = lax.rem(LANES - qs, LANES)
        patch = []
        for c in range(2):
            rolled = [
                pltpu.roll(band[c, qb + j, pl.ds(r, width), :], back_shift, 1)
                for j in range(wide + 1)
            ]
            patch.append(
                jnp.concatenate(
                    [jnp.where(near, rolled[j], rolled[j + 1]) for j in range(wide)], 1
                )
            )
        pr, pi = probe_ref[0], probe_ref[1]
        xr, xi = patch
        exit_wave = jnp.concatenate(
            [(pr * xr - pi * xi).astype(jnp.bfloat16), (pr * xi + pi * xr).astype(jnp.bfloat16)],
            1,
        )
        half = jnp.dot(exit_wave, fwd_ref[...], preferred_element_type=jnp.float32).astype(
            jnp.bfloat16
        )
        half = jnp.concatenate([half[:, :width], half[:, width:]], 0)
        far = jnp.dot(inv_ref[...], half, preferred_element_type=jnp.float32)
        fr, fi = far[:width], far[width:]
        misfit = fr * fr + fi * fi - frames_ref[i].astype(jnp.float32)
        back = jnp.concatenate(
            [(fr * misfit).astype(jnp.bfloat16), (fi * misfit).astype(jnp.bfloat16)], 0
        )
        mid = jnp.dot(fwd_ref[...], back, preferred_element_type=jnp.float32).astype(jnp.bfloat16)
        mid = jnp.concatenate([mid[:width], mid[width:]], 1)
        wave = jnp.dot(mid, inv_ref[...], preferred_element_type=jnp.float32)
        wr, wi = wave[:, :width], wave[:, width:]
        sums_ref[0] += xr * wr + xi * wi
        sums_ref[1] += xr * wi - xi * wr
        sums_ref[2] += xr * xr + xi * xi
        far_side = lane >= qs
        for c in range(2):
            grad = pr * wr + pi * wi if c == 0 else pr * wi - pi * wr
            grad = grad.astype(jnp.bfloat16).astype(jnp.float32)
            rolled = [
                pltpu.roll(grad[:, j * LANES : (j + 1) * LANES], qs, 1) for j in range(wide)
            ]
            zero = jnp.zeros_like(rolled[0])
            for j in range(wide + 1):
                here = rolled[j] if j < wide else zero
                before = rolled[j - 1] if j > 0 else zero
                total[c, qb + j, pl.ds(r, width), :] += jnp.where(far_side, here, before)
        return carry

    lax.fori_loop(0, count_ref[0, 0], one_frame, 0)
    for b in range(blocks):
        for c in range(2):
            for g in range(groups):
                out_refs[b][c, :, g * LANES : (g + 1) * LANES] = total[
                    c, g, pl.ds(b * rows, rows), :
                ].astype(out_refs[b].dtype)


def frame_sums(reach, positions, count, frames, blocks, probe):
    forward, inverse = dft_tables(probe.shape[-1])
    rows, columns = blocks[0].shape[1:]
    groups = columns // LANES
    n = len(blocks)
    vmem = pl.BlockSpec(memory_space=pltpu.VMEM)
    smem = pl.BlockSpec(memory_space=pltpu.SMEM)
    outs = [
        jax.ShapeDtypeStruct(blocks[0].shape, jnp.float32 if b == reach else jnp.bfloat16)
        for b in range(n)
    ] + [jax.ShapeDtypeStruct((3,) + probe.shape[1:], jnp.float32)]
    return pl.pallas_call(
        functools.partial(frames_kernel, reach),
        out_shape=outs,
        in_specs=[smem, smem, vmem] + [vmem] * (n + 3),
        out_specs=[vmem] * (n + 1),
        scratch_shapes=[
            pltpu.VMEM((2, groups + 1, n * rows, LANES), jnp.float32),
            pltpu.VMEM((2, groups + 1, n * rows, LANES), jnp.float32),
        ],
        compiler_params=pltpu.CompilerParams(vmem_limit_bytes=52 * 1024 * 1024),
    )(positions, count, frames, *blocks, probe, forward, inverse)


def shifted(block, offset, devices):
    pairs = [(p, p + offset) for p in range(devices) if 0 <= p + offset < devices]
    return lax.ppermute(block, "pos", pairs)


def local(devices, intensity, positions, counts, object_field, probe):
    width = probe.shape[-1]
    rows = object_field.shape[2]
    reach = width // rows
    own = object_field[0]
    blocks = [
        own if b == reach else shifted(own, reach - b, devices) for b in range(2 * reach + 1)
    ]
    *grads, sums = frame_sums(reach, positions[0], counts, intensity[0], blocks, probe)
    total = lax.psum(sums, ("tilt", "pos"))
    probe_grad = total[:2] / total[2:]
    object_grad = grads[reach]
    for b in range(2 * reach + 1):
        if b != reach:
            object_grad = object_grad + shifted(grads[b], b - reach, devices).astype(jnp.float32)
    return (object_grad[None], probe_grad)


def solution(mesh):
    placed = (
        P("tilt", "pos", None, None),
        P("tilt", "pos", None),
        P("tilt", "pos"),
        P("tilt", None, "pos", None),
        P(),
    )
    return jax.shard_map(
        functools.partial(local, mesh.shape["pos"]),
        mesh=mesh,
        in_specs=placed,
        out_specs=(P("tilt", None, "pos", None), P()),
        check_vma=False,
    )
```

time: 439 us -> 211 us (0.48)
  local copies, waits for them, and re-layouts: 144 us -> 1.73 us
  matrix products: 85.2 us -> 0 us
  waiting for transfers between devices: 81.4 us -> 147 us
  loops' own time: 60.4 us -> 0 us
  other arithmetic: 49.2 us -> 3.92 us
  starting transfers between devices: 0.12 us -> 25.8 us
  Pallas kernels: 0 us -> 16.9 us
    psum x1, waiting for transfers between devices: 0.02 us -> 137 us  [local(): total = lax.psum(sums, ('tilt', 'pos'))]
    dynamic_update_slice x48 -> x0, local copies, waits for them, and re-layouts: 89.2 us -> none  [the longest x16 75.5 us: add_one(): return lax.dynamic_update_slice(total, current + spread, start)]
    dot_general x34 -> x0, matrix products: 85.2 us -> none  [the longest x16 39.5 us: add_one(): jnp.einsum('crk,xk->crx', piece, picker, preferred_element_type=jnp.float32)]
    another operation x2 -> x0, loops' own time: 60.4 us -> none  [the longest x1 32.7 us: place_patches(): return lax.fori_loop(0, pieces.shape[0], add_one, total)]
    reduce_scatter x1 -> x0, waiting for transfers between devices: 51.9 us -> none  [local(): lax.psum_scatter(total[None], 'pos', scatter_dimension=2, tiled=True)]
    dynamic_slice x80 -> x0, local copies, waits for them, and re-layouts: 39.2 us -> none  [the longest x48 27.7 us: add_one(): piece = jnp.where(keep[index], pieces[index], jnp.zeros((), jnp.bfloat16))]
    all_gather x1 -> x0, waiting for transfers between devices: 28.7 us -> none  [local(): image = lax.all_gather(object_field, 'pos', axis=2, tiled=True)[0]]
    ppermute x0 -> x8, starting transfers between devices: none -> 25.7 us  [shifted(): return lax.ppermute(block, 'pos', pairs)]
  transfers between devices with their start and end apart: 3 -> 9, of which waited for: 2 -> 4; matrix products, arithmetic and copies ran while one was open for 40% -> 1% of each run, Pallas kernels for 0% -> 0%
where the time goes in v1:
time: 211 us; the launch traced here: 210 us
  waiting for transfers between devices  147 us (70%)
  starting transfers between devices  25.8 us (12%)
  Pallas kernels  16.9 us (8%)
  between operations  14.8 us (7%)
  other arithmetic  3.92 us (2%)
    psum x1, waiting for transfers between devices, local(): total = lax.psum(sums, ('tilt', 'pos'))  137 us
    ppermute x8, starting transfers between devices, shifted(): return lax.ppermute(block, 'pos', pairs)  25.7 us
    pallas_call x1, Pallas kernels, frame_sums(): pl.pallas_call(functools.partial(frames_kernel, reach), out_shape=outs, i...  16.9 us
    ppermute x8, waiting for transfers between devices, shifted(): return lax.ppermute(block, 'pos', pairs)  10.6 us
  transfers between devices with their start and end apart: 9, of which 4 were waited for; matrix products, arithmetic and copies ran while one was open for 1% of the time, Pallas kernels for 0%

profile of v1, /device:TPU:0, one launch (start us, length us, event | category | flops | bytes accessed | tf_op | source)
XLA Modules:
  0.0 210.3 jit_solution(13948829700560633693)
XLA Ops:
  7.2 0.0 all-reduce.2.cloned.1.call-start
  7.2 1.3 collective-permute-start.3
  8.5 1.3 collective-permute-start.2
  9.8 3.1 %collective-permute-start.1 = (bf16[2,96,768]{2,1,0:T(8,128)(2,1)}, bf16[2,96,768]{2,1,0:T(8,128)(2,1)S(1)}, u32[]{:S(2)}, u32[]{:S(2)}) collective-permute-start(bf16[2,96,768]{2,1,0:T(8,128)(2,1)} %bitcast.10), channel_id=1, source_target_pairs={{0,1},{1,2},{2,3},{3,4},{4,5},{5,6},{6,7},{8,9},{9,10},{10,11},{11... | collective-permute-start | bytes 884744 | tf_op jit(solution)/shard_map/ppermute | solution.py:150
  12.9 5.5 %collective-permute-start = (bf16[2,96,768]{2,1,0:T(8,128)(2,1)}, bf16[2,96,768]{2,1,0:T(8,128)(2,1)S(1)}, u32[]{:S(2)}, u32[]{:S(2)}) collective-permute-start(bf16[2,96,768]{2,1,0:T(8,128)(2,1)} %bitcast.11), channel_id=1, source_target_pairs={{0,2},{1,3},{2,4},{3,5},{4,6},{5,7},{8,10},{9,11},{10,12},{11,13},... | collective-permute-start | bytes 884744 | tf_op jit(solution)/shard_map/ppermute | solution.py:150
  19.0 0.8 copy.9.pos_ref
  19.8 0.0 collective-permute-done.3.refs_4_
  19.8 0.0 copy-start
  19.8 0.0 collective-permute-done.2.refs_3_
  19.8 0.0 copy-start.1
  19.8 0.0 collective-permute-done.1.refs_1_
  19.8 5.0 %collective-permute-done.refs_0_ = bf16[2,96,768]{2,1,0:T(8,128)(2,1)S(1)} collective-permute-done((bf16[2,96,768]{2,1,0:T(8,128)(2,1)}, bf16[2,96,768]{2,1,0:T(8,128)(2,1)S(1)}, u32[]{:S(2)}, u32[]{:S(2)}) %collective-permute-start) | collective-permute-done | bytes 294944 | tf_op jit(solution)/shard_map/ppermute | solution.py:150
  24.7 0.0 copy-done
  24.8 0.0 copy-done.1
  24.8 16.9 %shard_map.86 = (bf16[2,96,768]{2,1,0:T(8,128)(2,1)S(1)}, bf16[2,96,768]{2,1,0:T(8,128)(2,1)S(1)}, f32[2,96,768]{2,1,0:T(8,128)}, bf16[2,96,768]{2,1,0:T(8,128)(...) custom-call(s32[16,2]{1,0:T(8,128)S(1)} %copy.9.pos_ref, s32[1,1]{1,0:T(1,128)S(6)} %copy.11.count_ref, ...), custom_call_target="tpu_custom_call" | custom-call | tf_op jit(solution)/shard_map/pallas_call | solution.py:135
  41.6 1.3 collective-permute-start.4
  42.9 1.3 collective-permute-start.5
  44.2 4.2 %collective-permute-start.6 = (bf16[2,96,768]{2,1,0:T(8,128)(2,1)S(1)}, bf16[2,96,768]{2,1,0:T(8,128)(2,1)S(1)}, u32[]{:S(2)}, u32[]{:S(2)}) collective-permute-start(bf16[2,96,768]{2,1,0:T(8,128)(2,1)S(1)} %get-tuple-element.11), channel_id=1, source_target_pairs={{0,1},{1,2},{2,3},{3,4},{4,5},{5,6},{6,7},{8,9},{9,10},{10,11},{11... | collective-permute-start | bytes 884744 | tf_op jit(solution)/shard_map/ppermute | solution.py:150
  48.4 7.9 %collective-permute-start.7 = (bf16[2,96,768]{2,1,0:T(8,128)(2,1)S(1)}, bf16[2,96,768]{2,1,0:T(8,128)(2,1)S(1)}, u32[]{:S(2)}, u32[]{:S(2)}) collective-permute-start(bf16[2,96,768]{2,1,0:T(8,128)(2,1)S(1)} %get-tuple-element.12), channel_id=1, source_target_pairs={{0,2},{1,3},{2,4},{3,5},{4,6},{5,7},{8,10},{9,11},{10,12},{11,13},... | collective-permute-start | bytes 884744 | tf_op jit(solution)/shard_map/ppermute | solution.py:150
  56.3 0.0 all-reduce.2.cloned.1.call-update
  56.3 1.0 collective-permute-done.4
  57.3 0.0 collective-permute-done.5
  57.3 0.0 collective-permute-done.6
  57.3 4.6 %collective-permute-done.7 = bf16[2,96,768]{2,1,0:T(8,128)(2,1)S(1)} collective-permute-done((bf16[2,96,768]{2,1,0:T(8,128)(2,1)S(1)}, bf16[2,96,768]{2,1,0:T(8,128)(2,1)S(1)}, u32[]{:S(2)}, u32[]{:S(2)}) %collective-permute-start.7) | collective-permute-done | bytes 294944 | tf_op jit(solution)/shard_map/ppermute | solution.py:150
  61.9 2.0 add_bitcast_fusion
  63.9 136.7 %all-reduce.2.cloned.1.call-done = f32[3,256,256]{2,1,0:T(8,128)} async-done(((f32[3,256,256]{2,1,0:T(8,128)}), f32[3,256,256]{2,1,0:T(8,128)}) %all-reduce.2.cloned.1.call-update) | async-done | bytes 786448 | tf_op jit(solution)/shard_map/psum | solution.py:162
  200.6 1.0 slice_bitcast_fusion
  201.6 1.9 slice_divide_fusion
Async XLA Ops:
  7.2 193.5 %all-reduce.2.cloned.1.call-start = ((), (), s32[]{:S(2)}) async-start(), calls=%async_computation | async-start | bytes 1572864 | tf_op jit(solution)/shard_map/psum | solution.py:162
  7.2 12.6 %collective-permute-start.3 = (bf16[2,96,768]{2,1,0:T(8,128)(2,1)}, bf16[2,96,768]{2,1,0:T(8,128)(2,1)S(1)}, u32[]{:S(2)}, u32[]{:S(2)}) collective-permute-start(bf16[2,96,768]{2,1,0:T(8,128)(2,1)} %bitcast.8), channel_id=1, source_target_pairs={{2,0},{3,1},{4,2},{5,3},{6,4},{7,5},{10,8},{11,9},{12,10},{13,11},... | collective-permute-start | bytes 884744 | tf_op jit(solution)/shard_map/ppermute | solution.py:150
  8.5 11.3 %collective-permute-start.2 = (bf16[2,96,768]{2,1,0:T(8,128)(2,1)}, bf16[2,96,768]{2,1,0:T(8,128)(2,1)S(1)}, u32[]{:S(2)}, u32[]{:S(2)}) collective-permute-start(bf16[2,96,768]{2,1,0:T(8,128)(2,1)} %bitcast.9), channel_id=1, source_target_pairs={{1,0},{2,1},{3,2},{4,3},{5,4},{6,5},{7,6},{9,8},{10,9},{11,10},{12... | collective-permute-start | bytes 884744 | tf_op jit(solution)/shard_map/ppermute | solution.py:150
  9.8 10.0 %collective-permute-start.1 = (bf16[2,96,768]{2,1,0:T(8,128)(2,1)}, bf16[2,96,768]{2,1,0:T(8,128)(2,1)S(1)}, u32[]{:S(2)}, u32[]{:S(2)}) collective-permute-start(bf16[2,96,768]{2,1,0:T(8,128)(2,1)} %bitcast.10), channel_id=1, source_target_pairs={{0,1},{1,2},{2,3},{3,4},{4,5},{5,6},{6,7},{8,9},{9,10},{10,11},{11... | collective-permute-start | bytes 884744 | tf_op jit(solution)/shard_map/ppermute | solution.py:150
  12.9 11.9 %collective-permute-start = (bf16[2,96,768]{2,1,0:T(8,128)(2,1)}, bf16[2,96,768]{2,1,0:T(8,128)(2,1)S(1)}, u32[]{:S(2)}, u32[]{:S(2)}) collective-permute-start(bf16[2,96,768]{2,1,0:T(8,128)(2,1)} %bitcast.11), channel_id=1, source_target_pairs={{0,2},{1,3},{2,4},{3,5},{4,6},{5,7},{8,10},{9,11},{10,12},{11,13},... | collective-permute-start | bytes 884744 | tf_op jit(solution)/shard_map/ppermute | solution.py:150
  19.8 5.0 %copy-start = (bf16[2,96,768]{2,1,0:T(8,128)(2,1)}, bf16[2,96,768]{2,1,0:T(8,128)(2,1)S(1)}, u32[]{:S(2)}) copy-start(bf16[2,96,768]{2,1,0:T(8,128)(2,1)S(1)} %collective-permute-done.3.refs_4_) | copy-start | bytes 884740
  19.8 5.0 %copy-start.1 = (bf16[2,96,768]{2,1,0:T(8,128)(2,1)}, bf16[2,96,768]{2,1,0:T(8,128)(2,1)S(1)}, u32[]{:S(2)}) copy-start(bf16[2,96,768]{2,1,0:T(8,128)(2,1)S(1)} %collective-permute-done.2.refs_3_) | copy-start | bytes 884740
  41.6 15.6 %collective-permute-start.4 = (bf16[2,96,768]{2,1,0:T(8,128)(2,1)S(1)}, bf16[2,96,768]{2,1,0:T(8,128)(2,1)S(1)}, u32[]{:S(2)}, u32[]{:S(2)}) collective-permute-start(bf16[2,96,768]{2,1,0:T(8,128)(2,1)S(1)} %get-tuple-element.9), channel_id=1, source_target_pairs={{2,0},{3,1},{4,2},{5,3},{6,4},{7,5},{10,8},{11,9},{12,10},{13,11},... | collective-permute-start | bytes 884744 | tf_op jit(solution)/shard_map/ppermute | solution.py:150
  42.9 14.4 %collective-permute-start.5 = (bf16[2,96,768]{2,1,0:T(8,128)(2,1)S(1)}, bf16[2,96,768]{2,1,0:T(8,128)(2,1)S(1)}, u32[]{:S(2)}, u32[]{:S(2)}) collective-permute-start(bf16[2,96,768]{2,1,0:T(8,128)(2,1)S(1)} %get-tuple-element.10), channel_id=1, source_target_pairs={{1,0},{2,1},{3,2},{4,3},{5,4},{6,5},{7,6},{9,8},{10,9},{11,10},{12... | collective-permute-start | bytes 884744 | tf_op jit(solution)/shard_map/ppermute | solution.py:150
  44.2 13.1 %collective-permute-start.6 = (bf16[2,96,768]{2,1,0:T(8,128)(2,1)S(1)}, bf16[2,96,768]{2,1,0:T(8,128)(2,1)S(1)}, u32[]{:S(2)}, u32[]{:S(2)}) collective-permute-start(bf16[2,96,768]{2,1,0:T(8,128)(2,1)S(1)} %get-tuple-element.11), channel_id=1, source_target_pairs={{0,1},{1,2},{2,3},{3,4},{4,5},{5,6},{6,7},{8,9},{9,10},{10,11},{11... | collective-permute-start | bytes 884744 | tf_op jit(solution)/shard_map/ppermute | solution.py:150
  48.4 13.5 %collective-permute-start.7 = (bf16[2,96,768]{2,1,0:T(8,128)(2,1)S(1)}, bf16[2,96,768]{2,1,0:T(8,128)(2,1)S(1)}, u32[]{:S(2)}, u32[]{:S(2)}) collective-permute-start(bf16[2,96,768]{2,1,0:T(8,128)(2,1)S(1)} %get-tuple-element.12), channel_id=1, source_target_pairs={{0,2},{1,3},{2,4},{3,5},{4,6},{5,7},{8,10},{9,11},{10,12},{11,13},... | collective-permute-start | bytes 884744 | tf_op jit(solution)/shard_map/ppermute | solution.py:150
Sparse Core Ops, SparseCore 0:
  56.4 144.1 all-reduce.1

commit v2 on v1

--- a/solution.py
+++ b/solution.py
@@ -38,7 +38,8 @@
     probe_ref, fwd_ref, inv_ref = refs[blocks : blocks + 3]
     out_refs = refs[blocks + 3 : 2 * blocks + 3]
     sums_ref = refs[2 * blocks + 3]
-    band, total = refs[2 * blocks + 4 :]
+    chunks_ref = sums_ref
+    band, total, sums_ref = refs[2 * blocks + 4 :]
     rows = block_refs[0].shape[1]
     groups = block_refs[0].shape[2] // LANES
     width = probe_ref.shape[-1]
@@ -119,9 +120,15 @@
                 out_refs[b][c, :, g * LANES : (g + 1) * LANES] = total[
                     c, g, pl.ds(b * rows, rows), :
                 ].astype(out_refs[b].dtype)
-
-
-def frame_sums(reach, positions, count, frames, blocks, probe):
+    pairs, chips, tilts, _, chunk, _ = chunks_ref.shape
+    for e in range(pairs):
+        for c in range(chips):
+            for t in range(tilts):
+                start = ((e * chips + c) * tilts + t) * chunk
+                chunks_ref[e, c, t] = sums_ref[:, start : start + chunk, :]
+
+
+def frame_sums(reach, parts, positions, count, frames, blocks, probe):
     forward, inverse = dft_tables(probe.shape[-1])
     rows, columns = blocks[0].shape[1:]
     groups = columns // LANES
@@ -131,7 +138,7 @@
     outs = [
         jax.ShapeDtypeStruct(blocks[0].shape, jnp.float32 if b == reach else jnp.bfloat16)
         for b in range(n)
-    ] + [jax.ShapeDtypeStruct((3,) + probe.shape[1:], jnp.float32)]
+    ] + [jax.ShapeDtypeStruct(parts, jnp.float32)]
     return pl.pallas_call(
         functools.partial(frames_kernel, reach),
         out_shape=outs,
@@ -140,32 +147,284 @@
         scratch_shapes=[
             pltpu.VMEM((2, groups + 1, n * rows, LANES), jnp.float32),
             pltpu.VMEM((2, groups + 1, n * rows, LANES), jnp.float32),
+            pltpu.VMEM((3,) + probe.shape[1:], jnp.float32),
         ],
         compiler_params=pltpu.CompilerParams(vmem_limit_bytes=52 * 1024 * 1024),
     )(positions, count, frames, *blocks, probe, forward, inverse)
 
 
-def shifted(block, offset, devices):
-    pairs = [(p, p + offset) for p in range(devices) if 0 <= p + offset < devices]
-    return lax.ppermute(block, "pos", pairs)
-
-
-def local(devices, intensity, positions, counts, object_field, probe):
+def greet(tilts, devices):
+    t, p = lax.axis_index("tilt"), lax.axis_index("pos")
+    barrier = pltpu.get_barrier_semaphore()
+    for k in range(1, devices):
+        pl.semaphore_signal(
+            barrier,
+            inc=1,
+            device_id=(t, lax.rem(p + k, devices)),
+            device_id_type=pl.DeviceIdType.MESH,
+        )
+    for k in range(1, tilts):
+        pl.semaphore_signal(
+            barrier,
+            inc=1,
+            device_id=(lax.rem(t + k, tilts), p),
+            device_id_type=pl.DeviceIdType.MESH,
+        )
+    pl.semaphore_wait(barrier, devices - 1 + tilts - 1)
+
+
+def send(src, dst, sem_out, sem_in, tilt, pos):
+    return pltpu.make_async_remote_copy(
+        src_ref=src,
+        dst_ref=dst,
+        send_sem=sem_out,
+        recv_sem=sem_in,
+        device_id=(tilt, pos),
+        device_id_type=pl.DeviceIdType.MESH,
+    )
+
+
+def gather_kernel(devices, own_ref, *refs):
+    slots = {0: refs[0], 1: refs[1], 3: refs[2], 4: refs[3]}
+    out_sem, in_sem = refs[4:]
+    t, p = lax.axis_index("tilt"), lax.axis_index("pos")
+    chip, chips = p // 2, devices // 2
+    greet(1, devices)
+
+    def role(odd):
+        partner = p - 1 if odd else p + 1
+
+        def copy(src, slot, out, pos):
+            return send(src, slots[slot], out_sem.at[out], in_sem.at[slot], t, pos)
+
+        to_partner = copy(own_ref, 3 if odd else 1, 0, partner)
+        to_left = copy(own_ref, 4 if odd else 3, 1, 2 * chip - 1)
+        to_right = copy(own_ref, 1 if odd else 0, 2, 2 * chip + 2)
+        near, far = (3, 4) if odd else (1, 0)
+        forward = copy(slots[near], 4 if odd else 0, 3, partner)
+        from_partner = 1 if odd else 3
+        opposite = 0 if odd else 4
+        has_left, has_right = chip > 0, chip < chips - 1
+        outer, inner = (has_right, has_left) if odd else (has_left, has_right)
+
+        def arrived(slot):
+            copy(own_ref, slot, 0, partner).wait_recv()
+
+        pl.when(has_left)(to_left.start)
+        pl.when(has_right)(to_right.start)
+        to_partner.start()
+
+        @pl.when(outer)
+        def _():
+            arrived(near)
+            forward.start()
+            arrived(far)
+            forward.wait_send()
+
+        arrived(from_partner)
+        pl.when(inner)(lambda: arrived(opposite))
+        pl.when(has_left)(to_left.wait_send)
+        pl.when(has_right)(to_right.wait_send)
+        to_partner.wait_send()
+
+    pl.when(lax.rem(p, 2) == 0)(lambda: role(False))
+    pl.when(lax.rem(p, 2) == 1)(lambda: role(True))
+
+
+def gather(devices, own):
+    vmem = pl.BlockSpec(memory_space=pltpu.VMEM)
+    return pl.pallas_call(
+        functools.partial(gather_kernel, devices),
+        out_shape=[jax.ShapeDtypeStruct(own.shape, own.dtype)] * 4,
+        in_specs=[vmem],
+        out_specs=[vmem] * 4,
+        scratch_shapes=[pltpu.SemaphoreType.DMA((4,)), pltpu.SemaphoreType.DMA((5,))],
+        compiler_params=pltpu.CompilerParams(
+            collective_id=1, has_side_effects=True, vmem_limit_bytes=16 * 1024 * 1024
+        ),
+    )(own)
+
+
+def exchange_kernel(tilts, devices, *refs):
+    grads, sums = refs[:5], refs[5]
+    object_ref, probe_ref = refs[6:8]
+    mine, extra, from_left, from_right, near = refs[8:13]
+    half, plane, column, got0, got1, got2, result = refs[13:20]
+    obj_out, obj_in, out0, in0, out1, in1, out2, in2, out3, in3, out4, in4, out5, in5 = refs[20:]
+    t, p = lax.axis_index("tilt"), lax.axis_index("pos")
+    chip, chips = p // 2, devices // 2
+    e = lax.rem(p, 2)
+    partner = p + 1 - 2 * e
+    greet(tilts, devices)
+
+    swap = send(sums.at[1 - e], got0, out0.at[0], in0.at[0], t, partner)
+    swap.start()
+
+    def objects(odd, step):
+        has = chip < chips - 1 if odd else chip > 0
+        way = 1 if odd else -1
+        lands = from_left if odd else from_right
+        slot = 2 if odd else 3
+        far = send(grads[4 if odd else 0], lands, obj_out.at[2], obj_in.at[slot], t, p + 2 * way)
+        close = send(near, lands, obj_out.at[3], obj_in.at[slot], t, p + way)
+        to_extra = send(
+            grads[0 if odd else 4], extra, obj_out.at[0], obj_in.at[0], t, partner
+        )
+        to_mine = send(grads[1 if odd else 3], mine, obj_out.at[1], obj_in.at[1], t, partner)
+        if step == 0:
+            to_extra.start()
+            pl.when(has)(far.start)
+            to_mine.start()
+        elif step == 1:
+            to_extra.wait_recv()
+            near[...] = (
+                grads[3 if odd else 1][...].astype(jnp.float32) + extra[...].astype(jnp.float32)
+            ).astype(near.dtype)
+            pl.when(has)(close.start)
+        else:
+            to_mine.wait_recv()
+            to_extra.wait_send()
+            to_mine.wait_send()
+
+            @pl.when(has)
+            def _():
+                far.wait_send()
+                close.wait_send()
+
+    def both(step):
+        pl.when(e == 0)(lambda: objects(False, step))
+        pl.when(e == 1)(lambda: objects(True, step))
+
+    both(0)
+    swap.wait_recv()
+    half[...] = sums[e] + got0[...]
+    round1 = []
+    for k in range(1, chips):
+        other = lax.rem(chip + k, chips)
+        round1.append(
+            send(half.at[other], got1.at[k - 1], out1.at[k - 1], in1.at[k - 1], t, 2 * other + e)
+        )
+        round1[-1].start()
+    both(1)
+    total = half[chip]
+    for k in range(1, chips):
+        round1[k - 1].wait_recv()
+        total = total + got1[k - 1]
+    plane[...] = total
+    round2 = []
+    for k in range(1, tilts):
+        other = lax.rem(t + k, tilts)
+        round2.append(
+            send(plane.at[other], got2.at[k - 1], out2.at[k - 1], in2.at[k - 1], other, p)
+        )
+        round2[-1].start()
+    total = plane[t]
+    for k in range(1, tilts):
+        round2[k - 1].wait_recv()
+        total = total + got2[k - 1]
+    column[...] = total[:2] / total[2:]
+    result[e, chip, t] = column[...]
+    round3 = []
+    for k in range(1, tilts):
+        other = lax.rem(t + k, tilts)
+        round3.append(
+            send(column, result.at[e, chip, t], out3.at[k - 1], in3.at[k - 1], other, p)
+        )
+        round3[-1].start()
+    for k in range(1, tilts):
+        round3[k - 1].wait_recv()
+    round4 = []
+    for k in range(1, chips):
+        other = lax.rem(chip + k, chips)
+        round4.append(
+            send(
+                result.at[e, chip],
+                result.at[e, chip],
+                out4.at[k - 1],
+                in4.at[k - 1],
+                t,
+                2 * other + e,
+            )
+        )
+        round4[-1].start()
+    for k in range(1, chips):
+        round4[k - 1].wait_recv()
+    back = send(result.at[e], result.at[e], out5.at[0], in5.at[0], t, partner)
+    back.start()
+
+    both(2)
+    object_ref[0] = grads[2][...] + mine[...].astype(jnp.float32)
+
+    @pl.when(chip > 0)
+    def _():
+        send(near, from_left, obj_out.at[3], obj_in.at[2], t, partner).wait_recv()
+        object_ref[0] += from_left[...].astype(jnp.float32)
+
+    @pl.when(chip < chips - 1)
+    def _():
+        send(near, from_right, obj_out.at[3], obj_in.at[3], t, partner).wait_recv()
+        object_ref[0] += from_right[...].astype(jnp.float32)
+
+    back.wait_recv()
+    chunk = result.shape[-2]
+    for i in range(2):
+        for c in range(chips):
+            for s in range(tilts):
+                start = ((i * chips + c) * tilts + s) * chunk
+                probe_ref[:, start : start + chunk, :] = result[i, c, s]
+    swap.wait_send()
+    for copy in round1 + round2 + round3 + round4:
+        copy.wait_send()
+    back.wait_send()
+
+
+def exchange(tilts, devices, grads, sums):
+    vmem = pl.BlockSpec(memory_space=pltpu.VMEM)
+    _, chips, _, planes, chunk, width = sums.shape
+    block = grads[0].shape
+    dma = pltpu.SemaphoreType.DMA
+    f32 = jnp.float32
+    return pl.pallas_call(
+        functools.partial(exchange_kernel, tilts, devices),
+        out_shape=[
+            jax.ShapeDtypeStruct((1,) + block, f32),
+            jax.ShapeDtypeStruct((2, width, width), f32),
+        ],
+        in_specs=[vmem] * 6,
+        out_specs=[vmem] * 2,
+        scratch_shapes=[pltpu.VMEM(block, jnp.bfloat16)] * 5
+        + [
+            pltpu.VMEM((chips, tilts, planes, chunk, width), f32),
+            pltpu.VMEM((tilts, planes, chunk, width), f32),
+            pltpu.VMEM((2, chunk, width), f32),
+            pltpu.VMEM((chips, tilts, planes, chunk, width), f32),
+            pltpu.VMEM((chips - 1, tilts, planes, chunk, width), f32),
+            pltpu.VMEM((tilts - 1, planes, chunk, width), f32),
+            pltpu.VMEM((2, chips, tilts, 2, chunk, width), f32),
+        ]
+        + [dma((4,)), dma((4,))]
+        + [dma((1,))] * 2
+        + [dma((chips - 1,))] * 2
+        + [dma((tilts - 1,))] * 4
+        + [dma((chips - 1,))] * 2
+        + [dma((1,))] * 2,
+        compiler_params=pltpu.CompilerParams(
+            collective_id=2, has_side_effects=True, vmem_limit_bytes=40 * 1024 * 1024
+        ),
+    )(*grads, sums)
+
+
+def local(tilts, devices, intensity, positions, counts, object_field, probe):
     width = probe.shape[-1]
     rows = object_field.shape[2]
     reach = width // rows
+    assert reach == 2 and devices % 2 == 0
     own = object_field[0]
-    blocks = [
-        own if b == reach else shifted(own, reach - b, devices) for b in range(2 * reach + 1)
-    ]
-    *grads, sums = frame_sums(reach, positions[0], counts, intensity[0], blocks, probe)
-    total = lax.psum(sums, ("tilt", "pos"))
-    probe_grad = total[:2] / total[2:]
-    object_grad = grads[reach]
-    for b in range(2 * reach + 1):
-        if b != reach:
-            object_grad = object_grad + shifted(grads[b], b - reach, devices).astype(jnp.float32)
-    return (object_grad[None], probe_grad)
+    left2, left1, right1, right2 = gather(devices, own)
+    blocks = [left2, left1, own, right1, right2]
+    parts = (2, devices // 2, tilts, 3, width // (devices * tilts), width)
+    *grads, sums = frame_sums(reach, parts, positions[0], counts, intensity[0], blocks, probe)
+    return tuple(exchange(tilts, devices, grads, sums))
 
 
 def solution(mesh):
@@ -177,7 +436,7 @@
         P(),
     )
     return jax.shard_map(
-        functools.partial(local, mesh.shape["pos"]),
+        functools.partial(local, mesh.shape["tilt"], mesh.shape["pos"]),
         mesh=mesh,
         in_specs=placed,
         out_specs=(P("tilt", None, "pos", None), P()),

time: 211 us -> 88.8 us (0.42)
  waiting for transfers between devices: 147 us -> 0 us
  Pallas kernels: 16.9 us -> 80.4 us
  starting transfers between devices: 25.8 us -> 0 us
  between operations: 14.8 us -> 1.31 us
  local copies, waits for them, and re-layouts: 1.73 us -> 6.94 us
  other arithmetic: 3.92 us -> 0 us
    psum x1 -> x0, waiting for transfers between devices: 137 us -> none  [local(): total = lax.psum(sums, ('tilt', 'pos'))]
    pallas_call x0 -> x2, Pallas kernels: none -> 63.4 us  [the longest x1 50.2 us: exchange(): pl.pallas_call(functools.partial(exchange_kernel, tilts, devices), out_sh...]
    ppermute x8 -> x0, starting transfers between devices: 25.7 us -> none  [shifted(): return lax.ppermute(block, 'pos', pairs)]
    ppermute x8 -> x0, waiting for transfers between devices: 10.6 us -> none  [shifted(): return lax.ppermute(block, 'pos', pairs)]
    unnamed x4 -> x12, local copies, waits for them, and re-layouts: 0.01 us -> 6.18 us
  transfers between devices with their start and end apart: 9 -> 0, of which waited for: 4 -> 0; matrix products, arithmetic and copies ran while one was open for 1% -> 0% of each run, Pallas kernels for 0% -> 0%
where the time goes in v2:
time: 88.8 us; the launch traced here: 88.6 us
  Pallas kernels  80.4 us (91%)
  local copies, waits for them, and re-layouts  6.94 us (8%)
  between operations  1.31 us (1%)
    pallas_call x1, Pallas kernels, exchange(): pl.pallas_call(functools.partial(exchange_kernel, tilts, devices), out_sh...  50.2 us
    pallas_call x1, Pallas kernels, frame_sums(): pl.pallas_call(functools.partial(frames_kernel, reach), out_shape=outs, i...  17 us
    pallas_call x1, Pallas kernels, gather(): pl.pallas_call(functools.partial(gather_kernel, devices), out_shape=[jax....  13.2 us
    unnamed x12, local copies, waits for them, and re-layouts  6.18 us

profile of v2, /device:TPU:0, one launch (start us, length us, event | category | flops | bytes accessed | tf_op | source)
XLA Modules:
  0.0 88.6 jit_solution(15666717107975313523)
XLA Ops:
  1.3 0.8 copy.9.pos_ref
  2.0 0.0 copy-start
  2.0 1.0 %copy-done = bf16[1,2,96,768]{3,2,1,0:T(8,128)(2,1)S(1)} copy-done((bf16[1,2,96,768]{3,2,1,0:T(8,128)(2,1)S(1)}, bf16[1,2,96,768]{3,2,1,0:T(8,128)(2,1)}, u32[]{:S(2)}) %copy-start) | copy-done | bytes 294936
  3.0 13.2 %shard_map.86 = (bf16[2,96,768]{2,1,0:T(8,128)(2,1)S(1)}, bf16[2,96,768]{2,1,0:T(8,128)(2,1)S(1)}, bf16[2,96,768]{2,1,0:T(8,128)(2,1)S(1)}, bf16[2,96,768]{2,1,0:T(8,128)(2,1)S(1)}) custom-call(bf16[2,96,768]{2,1,0:T(8,128)(2,1)S(1)} %bitcast.4), custom_call_target="tpu_custom_call" | custom-call | tf_op jit(solution)/shard_map/pallas_call | solution.py:236
  16.2 0.0 copy-start.3
  16.2 0.7 copy-done.3
  16.9 0.0 copy-start.4
  16.9 0.7 copy-done.4
  17.6 17.0 %shard_map.87 = (bf16[2,96,768]{2,1,0:T(8,128)(2,1)S(1)}, bf16[2,96,768]{2,1,0:T(8,128)(2,1)S(1)}, f32[2,96,768]{2,1,0:T(8,128)}, bf16[2,96,768]{2,1,0:T(8,128)(...) custom-call(s32[16,2]{1,0:T(8,128)S(1)} %copy.9.pos_ref, s32[1,1]{1,0:T(1,128)S(6)} %copy.12.count_ref, ...), custom_call_target="tpu_custom_call" | custom-call | tf_op jit(solution)/shard_map/pallas_call | solution.py:142
  34.6 0.0 copy-start.1
  34.6 1.1 %copy-done.1 = f32[2,4,4,3,8,256]{5,4,3,2,1,0:T(8,128)S(1)} copy-done((f32[2,4,4,3,8,256]{5,4,3,2,1,0:T(8,128)S(1)}, f32[2,4,4,3,8,256]{5,4,3,2,1,0:T(8,128)}, u32[]{:S(2)}) %copy-start.1) | copy-done | bytes 786456
  35.7 0.0 copy-start.2
  35.7 1.1 %copy-done.2 = f32[2,96,768]{2,1,0:T(8,128)S(1)} copy-done((f32[2,96,768]{2,1,0:T(8,128)S(1)}, f32[2,96,768]{2,1,0:T(8,128)}, u32[]{:S(2)}) %copy-start.2) | copy-done | bytes 589848
  36.8 50.2 %shard_map.88 = (f32[1,2,96,768]{3,2,1,0:T(8,128)S(1)}, f32[2,256,256]{2,1,0:T(8,128)S(1)}) custom-call(bf16[2,96,768]{2,1,0:T(8,128)(2,1)S(1)} %get-tuple-element.16.refs_0_, bf16[2,96,768]{2,1,0:T(8,128)(2,1)S(1)} %get-tuple-element.17.refs_1_, f32[2,96,768]{2,1,0:T(8,128)S(1)} %copy-done.2, bf16[2,96,768]{2,1,0:T(8,128)(2,1)S(1)} %get-tuple-element.19.refs_3_, ...), custom_call_target="tpu_custom_call" | custom-call | tf_op jit(solution)/shard_map/pallas_call | solution.py:387
  87.0 0.8 copy.13
  87.8 0.8 copy.14
Async XLA Ops:
  2.0 1.0 %copy-start = (bf16[1,2,96,768]{3,2,1,0:T(8,128)(2,1)S(1)}, bf16[1,2,96,768]{3,2,1,0:T(8,128)(2,1)}, u32[]{:S(2)}) copy-start(bf16[1,2,96,768]{3,2,1,0:T(8,128)(2,1)} %param.10) | copy-start | bytes 884740
  16.2 0.7 copy-start.3
  16.9 0.7 copy-start.4
  34.6 1.1 %copy-start.1 = (f32[2,4,4,3,8,256]{5,4,3,2,1,0:T(8,128)S(1)}, f32[2,4,4,3,8,256]{5,4,3,2,1,0:T(8,128)}, u32[]{:S(2)}) copy-start(f32[2,4,4,3,8,256]{5,4,3,2,1,0:T(8,128)} %get-tuple-element.21.refs_5_) | copy-start | bytes 2359300
  35.7 1.1 %copy-start.2 = (f32[2,96,768]{2,1,0:T(8,128)S(1)}, f32[2,96,768]{2,1,0:T(8,128)}, u32[]{:S(2)}) copy-start(f32[2,96,768]{2,1,0:T(8,128)} %get-tuple-element.18.refs_2_) | copy-start | bytes 1769476

commit v3 on v2

--- a/solution.py
+++ b/solution.py
@@ -57,63 +57,95 @@
     sums_ref[...] = jnp.zeros_like(sums_ref)
     first = (lax.axis_index("pos") - reach) * rows
 
-    def one_frame(i, carry):
-        r = pos_ref[i, 0] - first
-        q = pos_ref[i, 1]
-        qb = q // LANES
-        qs = q % LANES
-        lane = lax.broadcasted_iota(jnp.int32, (width, LANES), 1)
-        near = lane < LANES - qs
-        back_shift = lax.rem(LANES - qs, LANES)
-        patch = []
-        for c in range(2):
-            rolled = [
-                pltpu.roll(band[c, qb + j, pl.ds(r, width), :], back_shift, 1)
-                for j in range(wide + 1)
-            ]
-            patch.append(
+    lane = lax.broadcasted_iota(jnp.int32, (width, LANES), 1)
+
+    def some_frames(at):
+        pr, pi = probe_ref[0], probe_ref[1]
+        spots, patches, exits = [], [], []
+        for i in at:
+            r = pos_ref[0, i] - first
+            q = pos_ref[1, i]
+            qb, qs = q // LANES, lax.rem(q, LANES)
+            spots.append((r, qb, qs))
+            near = lane < LANES - qs
+            back_shift = lax.rem(LANES - qs, LANES)
+            patch = []
+            for c in range(2):
+                rolled = [
+                    pltpu.roll(band[c, qb + j, pl.ds(r, width), :], back_shift, 1)
+                    for j in range(wide + 1)
+                ]
+                patch.append(
+                    jnp.concatenate(
+                        [jnp.where(near, rolled[j], rolled[j + 1]) for j in range(wide)], 1
+                    )
+                )
+            xr, xi = patch
+            patches.append((xr, xi))
+            exits.append(
                 jnp.concatenate(
-                    [jnp.where(near, rolled[j], rolled[j + 1]) for j in range(wide)], 1
+                    [
+                        (pr * xr - pi * xi).astype(jnp.bfloat16),
+                        (pr * xi + pi * xr).astype(jnp.bfloat16),
+                    ],
+                    1,
                 )
             )
-        pr, pi = probe_ref[0], probe_ref[1]
-        xr, xi = patch
-        exit_wave = jnp.concatenate(
-            [(pr * xr - pi * xi).astype(jnp.bfloat16), (pr * xi + pi * xr).astype(jnp.bfloat16)],
-            1,
-        )
-        half = jnp.dot(exit_wave, fwd_ref[...], preferred_element_type=jnp.float32).astype(
-            jnp.bfloat16
-        )
-        half = jnp.concatenate([half[:, :width], half[:, width:]], 0)
-        far = jnp.dot(inv_ref[...], half, preferred_element_type=jnp.float32)
-        fr, fi = far[:width], far[width:]
-        misfit = fr * fr + fi * fi - frames_ref[i].astype(jnp.float32)
-        back = jnp.concatenate(
-            [(fr * misfit).astype(jnp.bfloat16), (fi * misfit).astype(jnp.bfloat16)], 0
-        )
-        mid = jnp.dot(fwd_ref[...], back, preferred_element_type=jnp.float32).astype(jnp.bfloat16)
-        mid = jnp.concatenate([mid[:width], mid[width:]], 1)
-        wave = jnp.dot(mid, inv_ref[...], preferred_element_type=jnp.float32)
-        wr, wi = wave[:, :width], wave[:, width:]
-        sums_ref[0] += xr * wr + xi * wi
-        sums_ref[1] += xr * wi - xi * wr
-        sums_ref[2] += xr * xr + xi * xi
-        far_side = lane >= qs
-        for c in range(2):
-            grad = pr * wr + pi * wi if c == 0 else pr * wi - pi * wr
-            grad = grad.astype(jnp.bfloat16).astype(jnp.float32)
-            rolled = [
-                pltpu.roll(grad[:, j * LANES : (j + 1) * LANES], qs, 1) for j in range(wide)
-            ]
-            zero = jnp.zeros_like(rolled[0])
-            for j in range(wide + 1):
-                here = rolled[j] if j < wide else zero
-                before = rolled[j - 1] if j > 0 else zero
-                total[c, qb + j, pl.ds(r, width), :] += jnp.where(far_side, here, before)
-        return carry
-
-    lax.fori_loop(0, count_ref[0, 0], one_frame, 0)
+        halves = jnp.dot(
+            jnp.concatenate(exits, 0), fwd_ref[...], preferred_element_type=jnp.float32
+        ).astype(jnp.bfloat16)
+        mids = []
+        for n, i in enumerate(at):
+            half = halves[n * width : (n + 1) * width]
+            half = jnp.concatenate([half[:, :width], half[:, width:]], 0)
+            far = jnp.dot(inv_ref[...], half, preferred_element_type=jnp.float32)
+            fr, fi = far[:width], far[width:]
+            misfit = fr * fr + fi * fi - frames_ref[i].astype(jnp.float32)
+            back = jnp.concatenate(
+                [(fr * misfit).astype(jnp.bfloat16), (fi * misfit).astype(jnp.bfloat16)], 0
+            )
+            mid = jnp.dot(fwd_ref[...], back, preferred_element_type=jnp.float32).astype(
+                jnp.bfloat16
+            )
+            mids.append(jnp.concatenate([mid[:width], mid[width:]], 1))
+        waves = jnp.dot(
+            jnp.concatenate(mids, 0), inv_ref[...], preferred_element_type=jnp.float32
+        )
+        sums = [0.0, 0.0, 0.0]
+        for n, i in enumerate(at):
+            xr, xi = patches[n]
+            wave = waves[n * width : (n + 1) * width]
+            wr, wi = wave[:, :width], wave[:, width:]
+            sums[0] += xr * wr + xi * wi
+            sums[1] += xr * wi - xi * wr
+            sums[2] += xr * xr + xi * xi
+            r, qb, qs = spots[n]
+            far_side = lane >= qs
+            for c in range(2):
+                grad = pr * wr + pi * wi if c == 0 else pr * wi - pi * wr
+                grad = grad.astype(jnp.bfloat16).astype(jnp.float32)
+                rolled = [
+                    pltpu.roll(grad[:, j * LANES : (j + 1) * LANES], qs, 1)
+                    for j in range(wide)
+                ]
+                zero = jnp.zeros_like(rolled[0])
+                for j in range(wide + 1):
+                    here = rolled[j] if j < wide else zero
+                    before = rolled[j - 1] if j > 0 else zero
+                    total[c, qb + j, pl.ds(r, width), :] += jnp.where(far_side, here, before)
+        for k in range(3):
+            sums_ref[k] += sums[k]
+
+    count = count_ref[0, 0]
+
+    @pl.loop(0, count // 2)
+    def _(i):
+        some_frames([2 * i, 2 * i + 1])
+
+    @pl.when(lax.rem(count, 2) == 1)
+    def _():
+        some_frames([count - 1])
+
     for b in range(blocks):
         for c in range(2):
             for g in range(groups):
@@ -136,7 +168,7 @@
     vmem = pl.BlockSpec(memory_space=pltpu.VMEM)
     smem = pl.BlockSpec(memory_space=pltpu.SMEM)
     outs = [
-        jax.ShapeDtypeStruct(blocks[0].shape, jnp.float32 if b == reach else jnp.bfloat16)
+        jax.ShapeDtypeStruct(blocks[0].shape, jnp.float32)
         for b in range(n)
     ] + [jax.ShapeDtypeStruct(parts, jnp.float32)]
     return pl.pallas_call(
@@ -149,7 +181,7 @@
             pltpu.VMEM((2, groups + 1, n * rows, LANES), jnp.float32),
             pltpu.VMEM((3,) + probe.shape[1:], jnp.float32),
         ],
-        compiler_params=pltpu.CompilerParams(vmem_limit_bytes=52 * 1024 * 1024),
+        compiler_params=pltpu.CompilerParams(vmem_limit_bytes=32 * 1024 * 1024),
     )(positions, count, frames, *blocks, probe, forward, inverse)
 
 
@@ -239,8 +271,11 @@
         in_specs=[vmem],
         out_specs=[vmem] * 4,
         scratch_shapes=[pltpu.SemaphoreType.DMA((4,)), pltpu.SemaphoreType.DMA((5,))],
+        cost_estimate=pl.CostEstimate(
+            flops=0, bytes_accessed=64 * 1024 * 1024, transcendentals=0
+        ),
         compiler_params=pltpu.CompilerParams(
-            collective_id=1, has_side_effects=True, vmem_limit_bytes=16 * 1024 * 1024
+            collective_id=1, has_side_effects=True, vmem_limit_bytes=4 * 1024 * 1024
         ),
     )(own)
 
@@ -248,9 +283,9 @@
 def exchange_kernel(tilts, devices, *refs):
     grads, sums = refs[:5], refs[5]
     object_ref, probe_ref = refs[6:8]
-    mine, extra, from_left, from_right, near = refs[8:13]
-    half, plane, column, got0, got1, got2, result = refs[13:20]
-    obj_out, obj_in, out0, in0, out1, in1, out2, in2, out3, in3, out4, in4, out5, in5 = refs[20:]
+    mine, extra, from_left, from_right, near, distant = refs[8:14]
+    half, plane, column, got0, got1, got2, result = refs[14:21]
+    obj_out, obj_in, out0, in0, out1, in1, out2, in2, out3, in3, out4, in4, out5, in5 = refs[21:]
     t, p = lax.axis_index("tilt"), lax.axis_index("pos")
     chip, chips = p // 2, devices // 2
     e = lax.rem(p, 2)
@@ -258,14 +293,13 @@
     greet(tilts, devices)
 
     swap = send(sums.at[1 - e], got0, out0.at[0], in0.at[0], t, partner)
-    swap.start()
 
     def objects(odd, step):
         has = chip < chips - 1 if odd else chip > 0
         way = 1 if odd else -1
         lands = from_left if odd else from_right
         slot = 2 if odd else 3
-        far = send(grads[4 if odd else 0], lands, obj_out.at[2], obj_in.at[slot], t, p + 2 * way)
+        far = send(distant, lands, obj_out.at[2], obj_in.at[slot], t, p + 2 * way)
         close = send(near, lands, obj_out.at[3], obj_in.at[slot], t, p + way)
         to_extra = send(
             grads[0 if odd else 4], extra, obj_out.at[0], obj_in.at[0], t, partner
@@ -273,12 +307,14 @@
         to_mine = send(grads[1 if odd else 3], mine, obj_out.at[1], obj_in.at[1], t, partner)
         if step == 0:
             to_extra.start()
+            swap.start()
+            distant[...] = grads[4 if odd else 0][...].astype(distant.dtype)
             pl.when(has)(far.start)
             to_mine.start()
         elif step == 1:
             to_extra.wait_recv()
             near[...] = (
-                grads[3 if odd else 1][...].astype(jnp.float32) + extra[...].astype(jnp.float32)
+                grads[3 if odd else 1][...] + extra[...]
             ).astype(near.dtype)
             pl.when(has)(close.start)
         else:
@@ -353,7 +389,7 @@
     back.start()
 
     both(2)
-    object_ref[0] = grads[2][...] + mine[...].astype(jnp.float32)
+    object_ref[0] = grads[2][...] + mine[...]
 
     @pl.when(chip > 0)
     def _():
@@ -392,7 +428,8 @@
         ],
         in_specs=[vmem] * 6,
         out_specs=[vmem] * 2,
-        scratch_shapes=[pltpu.VMEM(block, jnp.bfloat16)] * 5
+        scratch_shapes=[pltpu.VMEM(block, f32)] * 2
+        + [pltpu.VMEM(block, jnp.bfloat16)] * 4
         + [
             pltpu.VMEM((chips, tilts, planes, chunk, width), f32),
             pltpu.VMEM((tilts, planes, chunk, width), f32),
@@ -409,7 +446,7 @@
         + [dma((chips - 1,))] * 2
         + [dma((1,))] * 2,
         compiler_params=pltpu.CompilerParams(
-            collective_id=2, has_side_effects=True, vmem_limit_bytes=40 * 1024 * 1024
+            collective_id=2, has_side_effects=True, vmem_limit_bytes=20 * 1024 * 1024
         ),
     )(*grads, sums)
 
@@ -423,7 +460,7 @@
     left2, left1, right1, right2 = gather(devices, own)
     blocks = [left2, left1, own, right1, right2]
     parts = (2, devices // 2, tilts, 3, width // (devices * tilts), width)
-    *grads, sums = frame_sums(reach, parts, positions[0], counts, intensity[0], blocks, probe)
+    *grads, sums = frame_sums(reach, parts, positions[0].T, counts, intensity[0], blocks, probe)
     return tuple(exchange(tilts, devices, grads, sums))
 
 

time: 88.8 us -> 82.1 us (0.925)
  Pallas kernels: 80.4 us -> 70.8 us
  local copies, waits for them, and re-layouts: 6.94 us -> 8.92 us
    pallas_call x1, Pallas kernels: 17 us -> 11.5 us  [frame_sums(): pl.pallas_call(functools.partial(frames_kernel, reach), out_shape=outs, i...]
    pallas_call x1, Pallas kernels: 50.2 us -> 46.1 us  [exchange(): pl.pallas_call(functools.partial(exchange_kernel, tilts, devices), out_sh...]
    unnamed x12 -> x16, local copies, waits for them, and re-layouts: 6.18 us -> 8.92 us
where the time goes in v3:
time: 82.1 us; the launch traced here: 81.1 us
  Pallas kernels  70.8 us (86%)
  local copies, waits for them, and re-layouts  8.92 us (11%)
  between operations  1.32 us (2%)
    pallas_call x1, Pallas kernels, exchange(): pl.pallas_call(functools.partial(exchange_kernel, tilts, devices), out_sh...  46.1 us
    pallas_call x1, Pallas kernels, gather(): pl.pallas_call(functools.partial(gather_kernel, devices), out_shape=[jax....  13.2 us
    pallas_call x1, Pallas kernels, frame_sums(): pl.pallas_call(functools.partial(frames_kernel, reach), out_shape=outs, i...  11.5 us
    unnamed x16, local copies, waits for them, and re-layouts  8.92 us

profile of v3, /device:TPU:0, one launch (start us, length us, event | category | flops | bytes accessed | tf_op | source)
XLA Modules:
  0.0 81.1 jit_solution(9538341642212304934)
XLA Ops:
  1.3 0.0 copy-start.1
  1.3 1.0 %copy-done.1 = bf16[1,2,96,768]{3,2,1,0:T(8,128)(2,1)S(1)} copy-done((bf16[1,2,96,768]{3,2,1,0:T(8,128)(2,1)S(1)}, bf16[1,2,96,768]{3,2,1,0:T(8,128)(2,1)}, u32[]{:S(2)}) %copy-start.1) | copy-done | bytes 294936
  2.2 13.2 %shard_map.86 = (bf16[2,96,768]{2,1,0:T(8,128)(2,1)S(1)}, bf16[2,96,768]{2,1,0:T(8,128)(2,1)S(1)}, bf16[2,96,768]{2,1,0:T(8,128)(2,1)S(1)}, bf16[2,96,768]{2,1,0:T(8,128)(2,1)S(1)}) custom-call(bf16[2,96,768]{2,1,0:T(8,128)(2,1)S(1)} %bitcast.6), custom_call_target="tpu_custom_call" | custom-call | bytes 67108864 | tf_op jit(solution)/shard_map/pallas_call | solution.py:268
  15.5 0.0 copy-start
  15.5 1.6 %copy-done = bf16[1,16,256,256]{3,2,1,0:T(8,128)(2,1)S(1)} copy-done((bf16[1,16,256,256]{3,2,1,0:T(8,128)(2,1)S(1)}, bf16[1,16,256,256]{3,2,1,0:T(8,128)(2,1)}, u32[]{:S(2)}) %copy-start) | copy-done | bytes 2097176
  17.1 0.0 copy-start.2
  17.1 1.0 %copy-done.2 = bf16[1,2,96,768]{3,2,1,0:T(8,128)(2,1)S(1)} copy-done((bf16[1,2,96,768]{3,2,1,0:T(8,128)(2,1)S(1)}, bf16[1,2,96,768]{3,2,1,0:T(8,128)(2,1)}, u32[]{:S(2)}) %copy-start.2) | copy-done | bytes 294936
  18.0 0.0 copy-start.3
  18.0 1.0 %copy-done.3 = f32[2,256,256]{2,1,0:T(8,128)S(1)} copy-done((f32[2,256,256]{2,1,0:T(8,128)S(1)}, f32[2,256,256]{2,1,0:T(8,128)}, u32[]{:S(2)}) %copy-start.3) | copy-done | bytes 524312
  19.1 0.0 copy-start.4
  19.1 1.0 %copy-done.4 = bf16[512,512]{1,0:T(8,128)(2,1)S(1)} copy-done((bf16[512,512]{1,0:T(8,128)(2,1)S(1)}, bf16[512,512]{1,0:T(8,128)(2,1)}, u32[]{:S(2)}) %copy-start.4) | copy-done | bytes 524312
  20.1 0.0 copy-start.5
  20.1 1.0 %copy-done.5 = bf16[512,512]{1,0:T(8,128)(2,1)S(1)} copy-done((bf16[512,512]{1,0:T(8,128)(2,1)S(1)}, bf16[512,512]{1,0:T(8,128)(2,1)}, u32[]{:S(2)}) %copy-start.5) | copy-done | bytes 524312
  21.2 0.0 copy-start.6
  21.2 0.7 copy-done.6
  21.8 11.5 %shard_map.87 = (f32[2,96,768]{2,1,0:T(8,128)S(1)}, f32[2,96,768]{2,1,0:T(8,128)S(1)}, f32[2,96,768]{2,1,0:T(8,128)S(1)}, f32[2,96,768]{2,1,0:T(8,128)S(1)}, f32...) custom-call(s32[2,16]{1,0:T(2,128)S(1)} %bitcast.8, s32[1,1]{1,0:T(1,128)S(6)} %copy.11.count_ref, ...), custom_call_target="tpu_custom_call" | custom-call | tf_op jit(solution)/shard_map/pallas_call | solution.py:174
  33.4 46.1 %shard_map.88 = (f32[1,2,96,768]{3,2,1,0:T(8,128)S(1)}, f32[2,256,256]{2,1,0:T(8,128)S(1)}) custom-call(f32[2,96,768]{2,1,0:T(8,128)S(1)} %get-tuple-element.16.refs_0_, f32[2,96,768]{2,1,0:T(8,128)S(1)} %get-tuple-element.17.refs_1_, f32[2,96,768]{2,1,0:T(8,128)S(1)} %get-tuple-element.18.refs_2_, f32[2,96,768]{2,1,0:T(8,128)S(1)} %get-tuple-element.19.refs_3_, ...), custom_call_target="tpu_custom_call" | custom-call | tf_op jit(solution)/shard_map/pallas_call | solution.py:423
  79.5 0.8 %copy.12 = f32[1,2,96,768]{3,2,1,0:T(8,128)} copy(f32[1,2,96,768]{3,2,1,0:T(8,128)S(1)} %get-tuple-element.24) | data formatting | bytes 1179648
  80.3 0.8 copy.13
Async XLA Ops:
  1.3 1.0 %copy-start.1 = (bf16[1,2,96,768]{3,2,1,0:T(8,128)(2,1)S(1)}, bf16[1,2,96,768]{3,2,1,0:T(8,128)(2,1)}, u32[]{:S(2)}) copy-start(bf16[1,2,96,768]{3,2,1,0:T(8,128)(2,1)} %param.10) | copy-start | bytes 884740
  15.5 1.6 %copy-start = (bf16[1,16,256,256]{3,2,1,0:T(8,128)(2,1)S(1)}, bf16[1,16,256,256]{3,2,1,0:T(8,128)(2,1)}, u32[]{:S(2)}) copy-start(bf16[1,16,256,256]{3,2,1,0:T(8,128)(2,1)} %param.7) | copy-start | bytes 6291460
  17.1 1.0 %copy-start.2 = (bf16[1,2,96,768]{3,2,1,0:T(8,128)(2,1)S(1)}, bf16[1,2,96,768]{3,2,1,0:T(8,128)(2,1)}, u32[]{:S(2)}) copy-start(bf16[1,2,96,768]{3,2,1,0:T(8,128)(2,1)} %param.10) | copy-start | bytes 884740
  18.0 1.0 %copy-start.3 = (f32[2,256,256]{2,1,0:T(8,128)S(1)}, f32[2,256,256]{2,1,0:T(8,128)}, u32[]{:S(2)}) copy-start(f32[2,256,256]{2,1,0:T(8,128)} %refs_5_.1) | copy-start | bytes 1572868
  19.1 1.0 %copy-start.4 = (bf16[512,512]{1,0:T(8,128)(2,1)S(1)}, bf16[512,512]{1,0:T(8,128)(2,1)}, u32[]{:S(2)}) copy-start(bf16[512,512]{1,0:T(8,128)(2,1)} %constant.11.refs_7_) | copy-start | bytes 1572868
  20.1 1.0 %copy-start.5 = (bf16[512,512]{1,0:T(8,128)(2,1)S(1)}, bf16[512,512]{1,0:T(8,128)(2,1)}, u32[]{:S(2)}) copy-start(bf16[512,512]{1,0:T(8,128)(2,1)} %constant.10.refs_6_) | copy-start | bytes 1572868
  21.2 0.7 copy-start.6
